TPU v7x, 512 devices: a whole 4x4x16 slice. The times are simulated.
512 devices in a mesh: stream: 16 (over z_lo, y), cross: 32 (over z_hi, x, core).
Axes of the slice: x: 4, y: 4, z: 16 (z_hi: 4, z_lo: 4; z = z_hi * 4 + z_lo), core: 2. Of those that a mesh axis runs over, the one named last changes fastest.
Arguments:
- vof: bfloat16 [6144, 512], P(('stream', 'cross')), may hold values from 0 to 1
- target: bfloat16 [6144, 512], P(('stream', 'cross')), may hold values from -21 to 21
- neighbours: int32 [6144, 26], P(('stream', 'cross')), may hold values from -1 to 6143, as said below
- live_blocks: int32 [512], P(('stream', 'cross')), may hold values from 2 to 12, as said below
- pick: int32 [512, 2], P(('stream', 'cross')), may hold values from -1 to 191, as said below
- w_first: bfloat16 [125, 128], replicated, may hold values from -0.5 to 0.5
- w_mid: bfloat16 [2, 128, 128], replicated, may hold values from -0.5 to 0.5
- w_last: bfloat16 [128], replicated, may hold values from -0.5 to 0.5
Outputs:
- prediction: float32 [4096, 512], P(('stream', 'cross'))
- grad_first: float32 [125, 128], replicated
- grad_mid: float32 [2, 128, 128], replicated
- grad_last: float32 [128], replicated
Inputs may be any that keep to these rules, and one draw needn't show every extreme that they name: Home slots 0 to live_blocks[d] - 1 of device d hold interface blocks and the rest are empty; in every slab 8 devices hold more than 6 blocks and the others at most 6. `neighbours`: an entry names a live home slot of a device whose stream index and cross index each differ from those of the block's own device by at most one. `pick`: in each slab every live home slot 6 + j of the device with cross index c is named, as c * 6 + j, by exactly one entry of one device of that slab; devices holding more than 6 blocks name none.
All inputs are finite; a program needn't handle non-finite values.
Results may differ from a plain program's by a relative error of at most 0.003.
The roundings to bfloat16 on the way count: a program that leaves them out, or rounds other values in their place, can miss the bound.
Values may be sent and summed in bfloat16 or wider, within the bound.
A program may use at most 128 MiB of HBM per device.

v0:
```python
import jax
import jax.numpy as jnp
from jax import lax
from jax.sharding import PartitionSpec as P

FEAT = 125
BE = 8
KEEP = 6
RECV = 2
PADROW = 1792


def from_behind(block, axis, distance):
    devices = range(lax.axis_size(axis))
    route = [(i - distance, i) for i in devices if i - distance in devices]
    return lax.ppermute(block, axis, route)


def assemble(center, border, block_edge):
    number = center.shape[0]
    pieces = jnp.concatenate([border[:, :13], center[:, None], border[:, 13:]], axis=1)
    shaped = pieces.reshape(number, 3, 3, 3, block_edge, block_edge, block_edge)
    shaped = shaped.transpose(0, 1, 4, 2, 5, 3, 6).reshape(
        number, 3 * block_edge, 3 * block_edge, 3 * block_edge
    )
    lower = block_edge - 2
    upper = 2 * block_edge + 2
    return shaped[:, lower:upper, lower:upper, lower:upper]


def stencil(padded, block_edge):
    columns = []
    for along_x in range(5):
        for along_y in range(5):
            for along_z in range(5):
                window = padded[
                    :,
                    along_x : along_x + block_edge,
                    along_y : along_y + block_edge,
                    along_z : along_z + block_edge,
                ]
                columns.append(window.reshape(-1))
    return jnp.stack(columns)


def contract_rows(former, latter):
    return lax.dot_general(
        former, latter, (((0,), (0,)), ((), ())), preferred_element_type=jnp.float32
    )


def contract_cols(former, latter):
    return lax.dot_general(
        former, latter, (((1,), (1,)), ((), ())), preferred_element_type=jnp.float32
    )


def train_terms(features, target_row, weight_mask, w_first, w_mid, w_last, loss_scale):
    hidden_one = jnp.tanh(contract_rows(w_first, features)).astype(jnp.bfloat16)
    hidden_two = jnp.tanh(contract_rows(w_mid[0], hidden_one)).astype(jnp.bfloat16)
    hidden_three = jnp.tanh(contract_rows(w_mid[1], hidden_two)).astype(jnp.bfloat16)
    predicted = jnp.dot(w_last, hidden_three, preferred_element_type=jnp.float32) * weight_mask
    residual = ((predicted - target_row.astype(jnp.float32)) * weight_mask / loss_scale).astype(
        jnp.bfloat16
    )
    grad_last = jnp.dot(hidden_three, residual, preferred_element_type=jnp.float32)
    slope_three = 1.0 - jnp.square(hidden_three.astype(jnp.float32))
    delta_three = (
        w_last.astype(jnp.float32)[:, None] * residual.astype(jnp.float32)[None, :] * slope_three
    ).astype(jnp.bfloat16)
    grad_third = contract_cols(hidden_two, delta_three)
    slope_two = 1.0 - jnp.square(hidden_two.astype(jnp.float32))
    delta_two = (
        jnp.dot(w_mid[1], delta_three, preferred_element_type=jnp.float32) * slope_two
    ).astype(jnp.bfloat16)
    grad_second = contract_cols(hidden_one, delta_two)
    slope_one = 1.0 - jnp.square(hidden_one.astype(jnp.float32))
    delta_one = (
        jnp.dot(w_mid[0], delta_two, preferred_element_type=jnp.float32) * slope_one
    ).astype(jnp.bfloat16)
    grad_first = contract_cols(features, delta_one)
    return (predicted, grad_first, jnp.stack([grad_second, grad_third]), grad_last)


def shards(vof, target, neighbours, live_blocks, pick, w_first, w_mid, w_last):
    home_blocks = vof.shape[0]
    cell_count = vof.shape[1]
    cross_size = lax.axis_size("cross")
    stream_size = lax.axis_size("stream")
    slab_index = lax.axis_index("stream")
    cross_index = lax.axis_index("cross")
    below = from_behind(vof, "stream", 1)
    above = from_behind(vof, "stream", -1)
    column = jnp.stack([below, vof, above])
    left = from_behind(column, "cross", 1)
    right = from_behind(column, "cross", -1)
    beside_all = jnp.stack([left, column, right], axis=1)
    table = jnp.concatenate(
        [beside_all.reshape(9 * home_blocks, cell_count), jnp.zeros((1, cell_count), vof.dtype)],
        axis=0,
    )
    owner_device = neighbours // home_blocks
    slab_step = owner_device // cross_size - slab_index + 1
    cross_step = owner_device % cross_size - cross_index + 1
    lookup = (slab_step * 3 + cross_step) * home_blocks + neighbours % home_blocks
    lookup = jnp.where(neighbours < 0, 9 * home_blocks, lookup)
    border = jnp.take(table, lookup, axis=0)
    padded = assemble(vof, border, BE)
    live_count = live_blocks[0]
    home_mask = (jnp.arange(home_blocks) < live_count).astype(jnp.float32)
    loss_scale = float(cell_count * KEEP * cross_size * stream_size)
    chosen = pick[0]
    padded_edge = padded.shape[1]
    flat_rows = padded.reshape(home_blocks, padded_edge**3)
    flat_rows = jnp.pad(flat_rows, ((0, 0), (0, PADROW - padded_edge**3)))
    pieces = (
        lax.all_gather(flat_rows[KEEP:], "cross", axis=0, tiled=True),
        lax.all_gather(target[KEEP:], "cross", axis=0, tiled=True),
    )
    selector = (chosen[:, None] == jnp.arange(pieces[0].shape[0])[None, :]).astype(jnp.bfloat16)
    got_blocks = jnp.dot(selector, pieces[0], preferred_element_type=jnp.float32)
    got_targets = jnp.dot(selector, pieces[1], preferred_element_type=jnp.float32)
    got_blocks = got_blocks.astype(jnp.bfloat16)
    got_targets = got_targets.astype(jnp.bfloat16)
    got_blocks = got_blocks[:, : padded_edge**3].reshape(
        RECV, padded_edge, padded_edge, padded_edge
    )
    work_padded = jnp.concatenate([padded[:KEEP], got_blocks], axis=0)
    work_target = jnp.concatenate([target[:KEEP], got_targets], axis=0)
    block_mask = jnp.concatenate([home_mask[:KEEP], (chosen >= 0).astype(jnp.float32)])
    predicted, grad_first, grad_mid, grad_last = train_terms(
        stencil(work_padded, BE),
        work_target.reshape(-1),
        jnp.repeat(block_mask, cell_count),
        w_first,
        w_mid,
        w_last,
        loss_scale,
    )
    prediction = predicted.reshape(KEEP + RECV, cell_count)
    hidden_size = grad_last.shape[0]
    packed = jnp.concatenate(
        [
            grad_first,
            grad_last[None, :],
            jnp.zeros((128 - FEAT - 1, hidden_size), jnp.float32),
            grad_mid.reshape(2 * hidden_size, hidden_size),
        ],
        axis=0,
    )
    summed = lax.psum(packed, ("stream", "cross"))
    return (
        prediction,
        summed[:FEAT],
        summed[128:].reshape(2, hidden_size, hidden_size),
        summed[FEAT],
    )


def solution(mesh):
    return jax.shard_map(
        shards,
        mesh=mesh,
        in_specs=(
            P(("stream", "cross"), None),
            P(("stream", "cross"), None),
            P(("stream", "cross"), None),
            P(("stream", "cross")),
            P(("stream", "cross"), None),
            P(),
            P(),
            P(),
        ),
        out_specs=(P(("stream", "cross"), None), P(), P(), P()),
        check_vma=False,
    )
```

profile of v0, /device:TPU:1, one launch (start us, length us, event | category | flops | bytes accessed | tf_op | source)
XLA Modules:
  0.0 796.8 jit_solution(742776914680141394)
XLA Ops:
  7.2 4.0 collective-permute-start
  11.3 1.3 collective-permute-start.1
  13.4 60.5 %all-gather.1 = bf16[32,6,512]{2,1,0:T(8,128)(2,1)S(1)} all-gather(bf16[1,6,512]{2,1,0:T(8,128)(2,1)S(1)} %get-tuple-element.139), channel_id=1, replica_groups=mesh['stream'=16,'cross'=32] {'cross'}, dimensions={0}, use_global_device_ids=true | all-gather | bytes 202752 | tf_op jit(solution)/shard_map/all_gather | solution.py:118
  77.8 1.9 collective-permute-start.2
  79.7 2.4 collective-permute-start.3
  84.1 1.2 convert_element_type.65
  86.1 2.0 gather_fusion
  88.6 7.5 reshape.47
  96.0 12.7 %copy.151 = bf16[12,3,8,3,8,3,8]{0,6,5,4,3,2,1:T(8,128)(2,1)} copy(bf16[12,3,8,3,8,3,8]{6,4,2,5,3,1,0:T(8,128)(2,1)} %bitcast.318) | data formatting | bytes 663552 | tf_op jit(solution)/shard_map/transpose | solution.py:23
  108.7 1.4 slice.565
  110.2 1.4 slice.564
  112.1 53.0 %all-gather = bf16[32,6,1792]{2,1,0:T(8,128)(2,1)S(1)} all-gather(bf16[1,6,1792]{2,1,0:T(8,128)(2,1)S(1)} %fusion.18), channel_id=1, replica_groups=mesh['stream'=16,'cross'=32] {'cross'}, dimensions={0}, use_global_device_ids=true | all-gather | bytes 709632 | tf_op jit(solution)/shard_map/all_gather | solution.py:117
  167.3 1.2 slice_maximum_fusion.12
  168.4 1.2 slice_maximum_fusion.13
  169.6 1.2 slice_maximum_fusion.14
  170.8 1.3 slice_maximum_fusion.15
  172.1 1.2 slice_maximum_fusion.16
  174.5 1.2 slice_maximum_fusion.18
  175.7 1.3 slice_maximum_fusion.19
  176.9 1.3 slice_maximum_fusion.20
  178.2 1.3 slice_maximum_fusion.21
  179.4 1.3 slice_maximum_fusion.22
  180.7 1.1 slice_maximum_fusion.23
  181.8 1.3 slice_maximum_fusion.24
  183.1 1.3 slice_maximum_fusion.25
  184.4 1.3 slice_maximum_fusion.26
  185.6 1.3 slice_maximum_fusion.27
  186.9 1.2 slice_maximum_fusion.28
  188.0 1.2 slice_maximum_fusion.29
  189.2 1.2 slice_maximum_fusion.11
  190.4 1.3 slice_maximum_fusion.10
  191.6 1.2 slice_maximum_fusion.9
  192.9 1.1 slice_maximum_fusion.8
  194.0 1.4 slice_maximum_fusion.7
  195.4 1.2 slice_maximum_fusion.6
  196.6 1.3 slice_maximum_fusion.5
  197.9 1.2 slice_maximum_fusion.4
  199.1 1.1 slice_maximum_fusion.3
  209.2 1.2 copy.200
  281.1 1.2 copy.191
  310.7 9.6 %stack.44 = bf16[125,4096]{1,0:T(8,128)(2,1)S(1)} concatenate(bf16[1,4096]{1,0:T(2,128)(2,1)S(1)} %stack_reshape.375, bf16[1,4096]{1,0:T(2,128)(2,1)S(1)} %stack_reshape.376, bf16[1,4096]{1,0:T(2,128)(2,1)S(1)} %stack_reshape.377, bf16[1,4096]{1,0:T(2,128)(2,1)S(1)} %stack_reshape.378, bf16[1,4096]{1,0:T(2,128)(2,1)S(1)} %stack_reshape.379, bf16[1,4096]{1,0:T(2,128)(2,1)S(1)} %stack_reshape.380, ...), dimensions={0} | concatenate | bytes 2048000 | tf_op jit(solution)/shard_map/stack | solution.py:43
  322.2 1.8 fusion.3
  324.0 2.1 fusion.6
  326.1 1.8 convolution_bitcast_fusion.1
  330.7 454.9 %all-reduce.4.cloned.1.call-done = f32[384,128]{1,0:T(8,128)} async-done(((f32[384,128]{1,0:T(8,128)}), f32[384,128]{1,0:T(8,128)}) %all-reduce.4.cloned.1.call-update) | async-done | bytes 196624 | tf_op jit(solution)/shard_map/psum | solution.py:151
  785.5 1.6 slice.816
  787.1 1.5 slice.815
  788.6 1.2 slice_bitcast_fusion.1
  (610 shorter events, 121.2 us)
Async XLA Ops:
  7.2 313.1 %copy-start = (bf16[125,128]{1,0:T(8,128)(2,1)S(1)}, bf16[125,128]{1,0:T(8,128)(2,1)}, u32[]{:S(2)}) copy-start(bf16[125,128]{1,0:T(8,128)(2,1)} %param.13) | copy-start | bytes 96004
  7.2 778.4 %all-reduce.4.cloned.1.call-start = ((), (), s32[]{:S(2)}) async-start(), calls=%async_computation | async-start | bytes 393216 | tf_op jit(solution)/shard_map/psum | solution.py:151
  7.2 69.8 %collective-permute-start = (bf16[12,512]{1,0:T(8,128)(2,1)}, bf16[12,512]{1,0:T(8,128)(2,1)S(1)}, u32[]{:S(2)}, u32[]{:S(2)}) collective-permute-start(bf16[12,512]{1,0:T(8,128)(2,1)} %param.8), channel_id=1, source_target_pairs={{0,32},{32,64},{64,96},{96,128},{128,160},{160,192},{192,224},{224... | collective-permute-start | bytes 36872 | tf_op jit(solution)/shard_map/ppermute | solution.py:16
  11.3 65.8 %collective-permute-start.1 = (bf16[12,512]{1,0:T(8,128)(2,1)}, bf16[12,512]{1,0:T(8,128)(2,1)S(1)}, u32[]{:S(2)}, u32[]{:S(2)}) collective-permute-start(bf16[12,512]{1,0:T(8,128)(2,1)} %param.8), channel_id=1, source_target_pairs={{32,0},{64,32},{96,64},{128,96},{160,128},{192,160},{224,192},{256... | collective-permute-start | bytes 36872 | tf_op jit(solution)/shard_map/ppermute | solution.py:16
  77.8 8.2 %collective-permute-start.2 = (bf16[3,12,512]{2,1,0:T(8,128)(2,1)S(1)}, bf16[3,12,512]{2,1,0:T(8,128)(2,1)S(1)}, u32[]{:S(2)}, u32[]{:S(2)}) collective-permute-start(bf16[3,12,512]{2,1,0:T(8,128)(2,1)S(1)} %get-tuple-element.137), channel_id=1, source_target_pairs={{0,1},{1,2},{2,3},{3,4},{4,5},{5,6},{6,7},{7,8},{8,9},{9,10},{10,1... | collective-permute-start | bytes 110600 | tf_op jit(solution)/shard_map/ppermute | solution.py:16
  79.7 6.2 collective-permute-start.3
  111.6 53.7 %copy-start.151 = (s32[1,2]{1,0:T(1,128)S(1)}, s32[1,2]{1,0:T(1,128)}, u32[]{:S(2)}) copy-start(s32[1,2]{1,0:T(1,128)} %param.12) | copy-start | bytes 28
  204.8 11.7 %copy-start.97 = (bf16[8,8,8,8]{0,3,2,1:T(8,128)(2,1)S(1)}, bf16[8,8,8,8]{0,3,2,1:T(8,128)(2,1)}, u32[]{:S(2)}) copy-start(bf16[8,8,8,8]{0,3,2,1:T(8,128)(2,1)} %get-tuple-element.79) | copy-start | bytes 24580
  205.2 12.3 %copy-start.96 = (bf16[8,8,8,8]{0,3,2,1:T(8,128)(2,1)S(1)}, bf16[8,8,8,8]{0,3,2,1:T(8,128)(2,1)}, u32[]{:S(2)}) copy-start(bf16[8,8,8,8]{0,3,2,1:T(8,128)(2,1)} %get-tuple-element.80) | copy-start | bytes 24580
  206.3 12.3 %copy-start.95 = (bf16[8,8,8,8]{0,3,2,1:T(8,128)(2,1)S(1)}, bf16[8,8,8,8]{0,3,2,1:T(8,128)(2,1)}, u32[]{:S(2)}) copy-start(bf16[8,8,8,8]{0,3,2,1:T(8,128)(2,1)} %get-tuple-element.81) | copy-start | bytes 24580
  207.4 12.3 %copy-start.94 = (bf16[8,8,8,8]{0,3,2,1:T(8,128)(2,1)S(1)}, bf16[8,8,8,8]{0,3,2,1:T(8,128)(2,1)}, u32[]{:S(2)}) copy-start(bf16[8,8,8,8]{0,3,2,1:T(8,128)(2,1)} %get-tuple-element.83) | copy-start | bytes 24580
  208.4 12.3 %copy-start.93 = (bf16[8,8,8,8]{0,3,2,1:T(8,128)(2,1)S(1)}, bf16[8,8,8,8]{0,3,2,1:T(8,128)(2,1)}, u32[]{:S(2)}) copy-start(bf16[8,8,8,8]{0,3,2,1:T(8,128)(2,1)} %get-tuple-element.84) | copy-start | bytes 24580
  210.4 11.5 %copy-start.92 = (bf16[8,8,8,8]{0,3,2,1:T(8,128)(2,1)S(1)}, bf16[8,8,8,8]{0,3,2,1:T(8,128)(2,1)}, u32[]{:S(2)}) copy-start(bf16[8,8,8,8]{0,3,2,1:T(8,128)(2,1)} %get-tuple-element.85) | copy-start | bytes 24580
  211.5 11.5 %copy-start.91 = (bf16[8,8,8,8]{0,3,2,1:T(8,128)(2,1)S(1)}, bf16[8,8,8,8]{0,3,2,1:T(8,128)(2,1)}, u32[]{:S(2)}) copy-start(bf16[8,8,8,8]{0,3,2,1:T(8,128)(2,1)} %get-tuple-element.87) | copy-start | bytes 24580
  212.5 11.5 %copy-start.90 = (bf16[8,8,8,8]{0,3,2,1:T(8,128)(2,1)S(1)}, bf16[8,8,8,8]{0,3,2,1:T(8,128)(2,1)}, u32[]{:S(2)}) copy-start(bf16[8,8,8,8]{0,3,2,1:T(8,128)(2,1)} %get-tuple-element.88) | copy-start | bytes 24580
  213.6 11.7 %copy-start.89 = (bf16[8,8,8,8]{0,3,2,1:T(8,128)(2,1)S(1)}, bf16[8,8,8,8]{0,3,2,1:T(8,128)(2,1)}, u32[]{:S(2)}) copy-start(bf16[8,8,8,8]{0,3,2,1:T(8,128)(2,1)} %get-tuple-element.89) | copy-start | bytes 24580
  214.7 11.7 %copy-start.88 = (bf16[8,8,8,8]{0,3,2,1:T(8,128)(2,1)S(1)}, bf16[8,8,8,8]{0,3,2,1:T(8,128)(2,1)}, u32[]{:S(2)}) copy-start(bf16[8,8,8,8]{0,3,2,1:T(8,128)(2,1)} %get-tuple-element.91) | copy-start | bytes 24580
  215.7 11.7 %copy-start.87 = (bf16[8,8,8,8]{0,3,2,1:T(8,128)(2,1)S(1)}, bf16[8,8,8,8]{0,3,2,1:T(8,128)(2,1)}, u32[]{:S(2)}) copy-start(bf16[8,8,8,8]{0,3,2,1:T(8,128)(2,1)} %get-tuple-element.92) | copy-start | bytes 24580
  216.8 11.7 %copy-start.86 = (bf16[8,8,8,8]{0,3,2,1:T(8,128)(2,1)S(1)}, bf16[8,8,8,8]{0,3,2,1:T(8,128)(2,1)}, u32[]{:S(2)}) copy-start(bf16[8,8,8,8]{0,3,2,1:T(8,128)(2,1)} %get-tuple-element.93) | copy-start | bytes 24580
  217.9 11.7 %copy-start.85 = (bf16[8,8,8,8]{0,3,2,1:T(8,128)(2,1)S(1)}, bf16[8,8,8,8]{0,3,2,1:T(8,128)(2,1)}, u32[]{:S(2)}) copy-start(bf16[8,8,8,8]{0,3,2,1:T(8,128)(2,1)} %get-tuple-element.95) | copy-start | bytes 24580
  218.9 11.6 %copy-start.84 = (bf16[8,8,8,8]{0,3,2,1:T(8,128)(2,1)S(1)}, bf16[8,8,8,8]{0,3,2,1:T(8,128)(2,1)}, u32[]{:S(2)}) copy-start(bf16[8,8,8,8]{0,3,2,1:T(8,128)(2,1)} %get-tuple-element.96) | copy-start | bytes 24580
  220.0 11.6 %copy-start.83 = (bf16[8,8,8,8]{0,3,2,1:T(8,128)(2,1)S(1)}, bf16[8,8,8,8]{0,3,2,1:T(8,128)(2,1)}, u32[]{:S(2)}) copy-start(bf16[8,8,8,8]{0,3,2,1:T(8,128)(2,1)} %get-tuple-element.97) | copy-start | bytes 24580
  221.1 11.6 %copy-start.82 = (bf16[8,8,8,8]{0,3,2,1:T(8,128)(2,1)S(1)}, bf16[8,8,8,8]{0,3,2,1:T(8,128)(2,1)}, u32[]{:S(2)}) copy-start(bf16[8,8,8,8]{0,3,2,1:T(8,128)(2,1)} %get-tuple-element.99) | copy-start | bytes 24580
  222.1 11.7 %copy-start.81 = (bf16[8,8,8,8]{0,3,2,1:T(8,128)(2,1)S(1)}, bf16[8,8,8,8]{0,3,2,1:T(8,128)(2,1)}, u32[]{:S(2)}) copy-start(bf16[8,8,8,8]{0,3,2,1:T(8,128)(2,1)} %get-tuple-element.100) | copy-start | bytes 24580
  223.2 11.6 %copy-start.80 = (bf16[8,8,8,8]{0,3,2,1:T(8,128)(2,1)S(1)}, bf16[8,8,8,8]{0,3,2,1:T(8,128)(2,1)}, u32[]{:S(2)}) copy-start(bf16[8,8,8,8]{0,3,2,1:T(8,128)(2,1)} %get-tuple-element.101) | copy-start | bytes 24580
  228.8 11.5 %copy-start.75 = (bf16[8,8,8,8]{0,3,2,1:T(8,128)(2,1)S(1)}, bf16[8,8,8,8]{0,3,2,1:T(8,128)(2,1)}, u32[]{:S(2)}) copy-start(bf16[8,8,8,8]{0,3,2,1:T(8,128)(2,1)} %get-tuple-element.108) | copy-start | bytes 24580
  230.9 11.5 %copy-start.73 = (bf16[8,8,8,8]{0,3,2,1:T(8,128)(2,1)S(1)}, bf16[8,8,8,8]{0,3,2,1:T(8,128)(2,1)}, u32[]{:S(2)}) copy-start(bf16[8,8,8,8]{0,3,2,1:T(8,128)(2,1)} %get-tuple-element.111) | copy-start | bytes 24580
  244.8 11.5 %copy-start.60 = (bf16[8,8,8,8]{0,3,2,1:T(8,128)(2,1)S(1)}, bf16[8,8,8,8]{0,3,2,1:T(8,128)(2,1)}, u32[]{:S(2)}) copy-start(bf16[8,8,8,8]{0,3,2,1:T(8,128)(2,1)} %get-tuple-element.128) | copy-start | bytes 24580
  245.8 11.5 %copy-start.59 = (bf16[8,8,8,8]{0,3,2,1:T(8,128)(2,1)S(1)}, bf16[8,8,8,8]{0,3,2,1:T(8,128)(2,1)}, u32[]{:S(2)}) copy-start(bf16[8,8,8,8]{0,3,2,1:T(8,128)(2,1)} %get-tuple-element.129) | copy-start | bytes 24580
  246.9 11.5 %copy-start.58 = (bf16[8,8,8,8]{0,3,2,1:T(8,128)(2,1)S(1)}, bf16[8,8,8,8]{0,3,2,1:T(8,128)(2,1)}, u32[]{:S(2)}) copy-start(bf16[8,8,8,8]{0,3,2,1:T(8,128)(2,1)} %get-tuple-element.131) | copy-start | bytes 24580
  248.0 11.5 %copy-start.57 = (bf16[8,8,8,8]{0,3,2,1:T(8,128)(2,1)S(1)}, bf16[8,8,8,8]{0,3,2,1:T(8,128)(2,1)}, u32[]{:S(2)}) copy-start(bf16[8,8,8,8]{0,3,2,1:T(8,128)(2,1)} %get-tuple-element.132) | copy-start | bytes 24580
  250.1 11.8 %copy-start.55 = (bf16[8,8,8,8]{0,3,2,1:T(8,128)(2,1)S(1)}, bf16[8,8,8,8]{0,3,2,1:T(8,128)(2,1)}, u32[]{:S(2)}) copy-start(bf16[8,8,8,8]{0,3,2,1:T(8,128)(2,1)} %get-tuple-element.130) | copy-start | bytes 24580
  251.2 11.8 %copy-start.54 = (bf16[8,8,8,8]{0,3,2,1:T(8,128)(2,1)S(1)}, bf16[8,8,8,8]{0,3,2,1:T(8,128)(2,1)}, u32[]{:S(2)}) copy-start(bf16[8,8,8,8]{0,3,2,1:T(8,128)(2,1)} %get-tuple-element.126) | copy-start | bytes 24580
  252.2 11.8 %copy-start.53 = (bf16[8,8,8,8]{0,3,2,1:T(8,128)(2,1)S(1)}, bf16[8,8,8,8]{0,3,2,1:T(8,128)(2,1)}, u32[]{:S(2)}) copy-start(bf16[8,8,8,8]{0,3,2,1:T(8,128)(2,1)} %get-tuple-element.122) | copy-start | bytes 24580
  253.3 11.8 %copy-start.52 = (bf16[8,8,8,8]{0,3,2,1:T(8,128)(2,1)S(1)}, bf16[8,8,8,8]{0,3,2,1:T(8,128)(2,1)}, u32[]{:S(2)}) copy-start(bf16[8,8,8,8]{0,3,2,1:T(8,128)(2,1)} %get-tuple-element.118) | copy-start | bytes 24580
  254.4 11.8 %copy-start.51 = (bf16[8,8,8,8]{0,3,2,1:T(8,128)(2,1)S(1)}, bf16[8,8,8,8]{0,3,2,1:T(8,128)(2,1)}, u32[]{:S(2)}) copy-start(bf16[8,8,8,8]{0,3,2,1:T(8,128)(2,1)} %get-tuple-element.114) | copy-start | bytes 24580
  255.4 11.8 %copy-start.50 = (bf16[8,8,8,8]{0,3,2,1:T(8,128)(2,1)S(1)}, bf16[8,8,8,8]{0,3,2,1:T(8,128)(2,1)}, u32[]{:S(2)}) copy-start(bf16[8,8,8,8]{0,3,2,1:T(8,128)(2,1)} %get-tuple-element.110) | copy-start | bytes 24580
  256.5 11.8 %copy-start.49 = (bf16[8,8,8,8]{0,3,2,1:T(8,128)(2,1)S(1)}, bf16[8,8,8,8]{0,3,2,1:T(8,128)(2,1)}, u32[]{:S(2)}) copy-start(bf16[8,8,8,8]{0,3,2,1:T(8,128)(2,1)} %get-tuple-element.106) | copy-start | bytes 24580
  257.6 11.8 %copy-start.48 = (bf16[8,8,8,8]{0,3,2,1:T(8,128)(2,1)S(1)}, bf16[8,8,8,8]{0,3,2,1:T(8,128)(2,1)}, u32[]{:S(2)}) copy-start(bf16[8,8,8,8]{0,3,2,1:T(8,128)(2,1)} %get-tuple-element.102) | copy-start | bytes 24580
  258.6 11.8 %copy-start.47 = (bf16[8,8,8,8]{0,3,2,1:T(8,128)(2,1)S(1)}, bf16[8,8,8,8]{0,3,2,1:T(8,128)(2,1)}, u32[]{:S(2)}) copy-start(bf16[8,8,8,8]{0,3,2,1:T(8,128)(2,1)} %get-tuple-element.98) | copy-start | bytes 24580
  259.7 11.8 %copy-start.46 = (bf16[8,8,8,8]{0,3,2,1:T(8,128)(2,1)S(1)}, bf16[8,8,8,8]{0,3,2,1:T(8,128)(2,1)}, u32[]{:S(2)}) copy-start(bf16[8,8,8,8]{0,3,2,1:T(8,128)(2,1)} %get-tuple-element.94) | copy-start | bytes 24580
  262.2 11.5 %copy-start.37 = (bf16[8,8,8,8]{0,3,2,1:T(8,128)(2,1)S(1)}, bf16[8,8,8,8]{0,3,2,1:T(8,128)(2,1)}, u32[]{:S(2)}) copy-start(bf16[8,8,8,8]{0,3,2,1:T(8,128)(2,1)} %get-tuple-element.86) | copy-start | bytes 24580
  264.3 11.5 %copy-start.28 = (bf16[8,8,8,8]{0,3,2,1:T(8,128)(2,1)S(1)}, bf16[8,8,8,8]{0,3,2,1:T(8,128)(2,1)}, u32[]{:S(2)}) copy-start(bf16[8,8,8,8]{0,3,2,1:T(8,128)(2,1)} %get-tuple-element.78) | copy-start | bytes 24580
  266.5 11.5 %copy-start.20 = (bf16[8,8,8,8]{0,3,2,1:T(8,128)(2,1)S(1)}, bf16[8,8,8,8]{0,3,2,1:T(8,128)(2,1)}, u32[]{:S(2)}) copy-start(bf16[8,8,8,8]{0,3,2,1:T(8,128)(2,1)} %get-tuple-element.70) | copy-start | bytes 24580
  267.6 11.5 %copy-start.15 = (bf16[8,8,8,8]{0,3,2,1:T(8,128)(2,1)S(1)}, bf16[8,8,8,8]{0,3,2,1:T(8,128)(2,1)}, u32[]{:S(2)}) copy-start(bf16[8,8,8,8]{0,3,2,1:T(8,128)(2,1)} %get-tuple-element.66) | copy-start | bytes 24580
  268.6 11.5 %copy-start.11 = (bf16[8,8,8,8]{0,3,2,1:T(8,128)(2,1)S(1)}, bf16[8,8,8,8]{0,3,2,1:T(8,128)(2,1)}, u32[]{:S(2)}) copy-start(bf16[8,8,8,8]{0,3,2,1:T(8,128)(2,1)} %get-tuple-element.62) | copy-start | bytes 24580
  270.8 12.4 %copy-start.45 = (bf16[8,8,8,8]{0,3,2,1:T(8,128)(2,1)S(1)}, bf16[8,8,8,8]{0,3,2,1:T(8,128)(2,1)}, u32[]{:S(2)}) copy-start(bf16[8,8,8,8]{0,3,2,1:T(8,128)(2,1)} %get-tuple-element.60) | copy-start | bytes 24580
  271.8 11.8 %copy-start.44 = (bf16[8,8,8,8]{0,3,2,1:T(8,128)(2,1)S(1)}, bf16[8,8,8,8]{0,3,2,1:T(8,128)(2,1)}, u32[]{:S(2)}) copy-start(bf16[8,8,8,8]{0,3,2,1:T(8,128)(2,1)} %get-tuple-element.61) | copy-start | bytes 24580
  (111 other events, 775.7 us)
Sparse Core Ops, SparseCore 0:
  330.2 455.2 all-reduce.3
where the time goes:
time: 803 us; the launch traced here: 797 us
  waiting for transfers between devices  455 us (57%)
  local copies, waits for them, and re-layouts  152 us (19%)
  blocking collectives  114 us (14%)
  other arithmetic  39.4 us (5%)
  between operations  17.8 us (2%)
  matrix products  9.76 us (1%)
  starting transfers between devices  9.69 us (1%)
    psum x1, waiting for transfers between devices, shards(): summed = lax.psum(packed, ('stream', 'cross'))  455 us
    another operation x126, local copies, waits for them, and re-layouts, stencil(): return jnp.stack(columns)  77.5 us
    all_gather x1, blocking collectives, shards(): lax.all_gather(target[KEEP:], 'cross', axis=0, tiled=True)  60.5 us
    all_gather x1, blocking collectives, shards(): lax.all_gather(flat_rows[KEEP:], 'cross', axis=0, tiled=True)  53 us
    slice x125, local copies, waits for them, and re-layouts, stencil(): padded[:, along_x:along_x + block_edge, along_y:along_y + block_edge, alo...  38.1 us
    concatenate x31, other arithmetic, shards(): work_padded = jnp.concatenate([padded[:KEEP], got_blocks], axis=0)  34.8 us
  transfers between devices with their start and end apart: 5, of which 1 were waited for; matrix products, arithmetic and copies ran while one was open for 1% of the time, Pallas kernels for 0%

commit v1 on v0

--- a/solution.py
+++ b/solution.py
@@ -8,6 +8,11 @@
 KEEP = 6
 RECV = 2
 PADROW = 1792
+
+
+def add_all(x, axis):
+    shards = lax.all_gather(x, axis)
+    return jnp.sum(shards, axis=0)
 
 
 def from_behind(block, axis, distance):
@@ -148,7 +153,7 @@
         ],
         axis=0,
     )
-    summed = lax.psum(packed, ("stream", "cross"))
+    summed = add_all(packed, ("stream", "cross"))
     return (
         prediction,
         summed[:FEAT],

time: 803 us -> 1360 us (1.69)
  waiting for transfers between devices: 455 us -> 940 us
  local copies, waits for them, and re-layouts: 152 us -> 194 us
  other arithmetic: 39.4 us -> 70.2 us
    all_gather x0 -> x1, waiting for transfers between devices: none -> 940 us  [add_all(): shards = lax.all_gather(x, axis)]
    psum x1 -> x0, waiting for transfers between devices: 455 us -> none  [shards(): summed = lax.psum(packed, ('stream', 'cross'))]
    reduce_sum x0 -> x1, other arithmetic: none -> 30.9 us  [add_all(): return jnp.sum(shards, axis=0)]
    slice x125, local copies, waits for them, and re-layouts: 38.1 us -> 65.4 us  [stencil(): padded[:, along_x:along_x + block_edge, along_y:along_y + block_edge, alo...]
    another operation x126, local copies, waits for them, and re-layouts: 77.5 us -> 94.4 us  [stencil(): return jnp.stack(columns)]
where the time goes in v1:
time: 1360 us; the launch traced here: 1350 us
  waiting for transfers between devices  940 us (69%)
  local copies, waits for them, and re-layouts  194 us (14%)
  blocking collectives  111 us (8%)
  other arithmetic  70.2 us (5%)
  between operations  17.8 us (1%)
    all_gather x1, waiting for transfers between devices, add_all(): shards = lax.all_gather(x, axis)  940 us
    another operation x126, local copies, waits for them, and re-layouts, stencil(): return jnp.stack(columns)  94.4 us
    slice x125, local copies, waits for them, and re-layouts, stencil(): padded[:, along_x:along_x + block_edge, along_y:along_y + block_edge, alo...  65.4 us
    all_gather x1, blocking collectives, shards(): lax.all_gather(target[KEEP:], 'cross', axis=0, tiled=True)  60.5 us
    all_gather x1, blocking collectives, shards(): lax.all_gather(flat_rows[KEEP:], 'cross', axis=0, tiled=True)  50.4 us
    concatenate x31, other arithmetic, shards(): work_padded = jnp.concatenate([padded[:KEEP], got_blocks], axis=0)  34.7 us
    reduce_sum x1, other arithmetic, add_all(): return jnp.sum(shards, axis=0)  30.9 us
  transfers between devices with their start and end apart: 5, of which 1 were waited for; matrix products, arithmetic and copies ran while one was open for 1% of the time, Pallas kernels for 0%

profile of v1, /device:TPU:1, one launch (start us, length us, event | category | flops | bytes accessed | tf_op | source)
XLA Modules:
  0.0 1353.1 jit_solution(5195124274105249857)
XLA Ops:
  7.2 4.0 collective-permute-start
  11.3 1.3 collective-permute-start.1
  14.8 60.5 %all-gather.2 = bf16[32,6,512]{2,1,0:T(8,128)(2,1)S(1)} all-gather(bf16[1,6,512]{2,1,0:T(8,128)(2,1)S(1)} %get-tuple-element.139), channel_id=1, replica_groups=mesh['stream'=16,'cross'=32] {'cross'}, dimensions={0}, use_global_device_ids=true | all-gather | bytes 202752 | tf_op jit(solution)/shard_map/all_gather | solution.py:123
  77.8 2.1 collective-permute-start.3
  79.9 3.5 collective-permute-start.2
  87.3 2.0 gather_fusion
  89.8 7.4 reshape.47
  97.2 12.7 copy.151
  110.0 1.4 slice.564
  111.4 1.4 slice.565
  113.3 50.4 %all-gather.1 = bf16[32,6,1792]{2,1,0:T(8,128)(2,1)S(1)} all-gather(bf16[1,6,1792]{2,1,0:T(8,128)(2,1)S(1)} %fusion.18), channel_id=1, replica_groups=mesh['stream'=16,'cross'=32] {'cross'}, dimensions={0}, use_global_device_ids=true | all-gather | bytes 709632 | tf_op jit(solution)/shard_map/all_gather | solution.py:122
  167.6 1.2 slice_maximum_fusion.27
  168.8 1.2 slice_maximum_fusion.26
  170.1 1.3 slice_maximum_fusion.25
  171.4 1.2 slice_maximum_fusion.24
  172.6 1.2 slice_maximum_fusion.23
  173.8 1.2 slice_maximum_fusion.22
  175.0 1.2 slice_maximum_fusion.21
  176.2 1.3 slice_maximum_fusion.20
  177.5 1.2 slice_maximum_fusion.19
  181.0 1.2 slice_maximum_fusion.16
  182.2 1.3 slice_maximum_fusion.15
  183.6 1.3 slice_maximum_fusion.14
  187.2 1.2 slice_maximum_fusion.11
  188.4 1.2 slice_maximum_fusion.10
  189.6 1.2 slice_maximum_fusion.9
  192.0 1.2 slice_maximum_fusion.7
  193.2 1.4 slice_maximum_fusion.6
  194.6 1.2 slice_maximum_fusion.5
  195.8 1.2 slice_maximum_fusion.4
  200.1 1.2 copy.248
  201.5 1.2 copy.245
  202.9 1.2 copy.246
  204.2 1.2 copy.247
  205.6 1.2 copy.249
  209.0 1.2 copy.250
  210.9 1.2 copy.239
  212.9 1.2 copy.240
  223.4 1.2 copy.235
  238.0 1.2 copy.225
  239.9 1.2 copy.226
  241.9 1.2 copy.256
  351.6 11.4 stack.44
  365.9 1.8 fusion.3
  367.7 2.1 fusion.6
  369.8 1.7 convolution_bitcast_fusion.1
  373.2 940.1 %all-gather.5.cloned.1.call-done = f32[196608,128]{1,0:T(8,128)} async-done(((f32[384,128]{1,0:T(8,128)}), f32[196608,128]{1,0:T(8,128)}) %all-gather.5.cloned.1.call-update) | async-done | bytes 100663312 | tf_op jit(solution)/shard_map/all_gather | solution.py:14
  1313.3 30.9 %reduce_sum.9 = f32[384,128]{1,0:T(8,128)S(1)} reduce(f32[512,384,128]{2,1,0:T(8,128)} %bitcast.22, f32[]{:T(128)} %constant.82.clone.1), dimensions={0}, to_apply=%region_0.1 | reduce | flops 25116672 | bytes 100859904 | tf_op jit(solution)/shard_map/reduce_sum | solution.py:15
  (545 shorter events, 162.8 us)
Async XLA Ops:
  7.2 355.8 %copy-start = (bf16[125,128]{1,0:T(8,128)(2,1)S(1)}, bf16[125,128]{1,0:T(8,128)(2,1)}, u32[]{:S(2)}) copy-start(bf16[125,128]{1,0:T(8,128)(2,1)} %param.13) | copy-start | bytes 96004
  7.2 1306.1 %all-gather.5.cloned.1.call-start = ((), (), s32[]{:S(2)}) async-start(), calls=%async_computation | async-start | bytes 100859904 | tf_op jit(solution)/shard_map/all_gather | solution.py:14
  7.2 69.8 %collective-permute-start = (bf16[12,512]{1,0:T(8,128)(2,1)}, bf16[12,512]{1,0:T(8,128)(2,1)S(1)}, u32[]{:S(2)}, u32[]{:S(2)}) collective-permute-start(bf16[12,512]{1,0:T(8,128)(2,1)} %param.8), channel_id=1, source_target_pairs={{0,32},{32,64},{64,96},{96,128},{128,160},{160,192},{192,224},{224... | collective-permute-start | bytes 36872 | tf_op jit(solution)/shard_map/ppermute | solution.py:21
  11.3 65.8 %collective-permute-start.1 = (bf16[12,512]{1,0:T(8,128)(2,1)}, bf16[12,512]{1,0:T(8,128)(2,1)S(1)}, u32[]{:S(2)}, u32[]{:S(2)}) collective-permute-start(bf16[12,512]{1,0:T(8,128)(2,1)} %param.8), channel_id=1, source_target_pairs={{32,0},{64,32},{96,64},{128,96},{160,128},{192,160},{224,192},{256... | collective-permute-start | bytes 36872 | tf_op jit(solution)/shard_map/ppermute | solution.py:21
  77.8 9.4 collective-permute-start.3
  79.9 7.3 collective-permute-start.2
  112.8 51.1 %copy-start.118 = (s32[1,2]{1,0:T(1,128)S(1)}, s32[1,2]{1,0:T(1,128)}, u32[]{:S(2)}) copy-start(s32[1,2]{1,0:T(1,128)} %param.12) | copy-start | bytes 28
  208.2 14.1 %copy-start.65 = (bf16[8,8,8,8]{0,3,2,1:T(8,128)(2,1)S(1)}, bf16[8,8,8,8]{0,3,2,1:T(8,128)(2,1)}, u32[]{:S(2)}) copy-start(bf16[8,8,8,8]{0,3,2,1:T(8,128)(2,1)} %get-tuple-element.116) | copy-start | bytes 24580
  218.3 14.3 %copy-start.61 = (bf16[8,8,8,8]{0,3,2,1:T(8,128)(2,1)S(1)}, bf16[8,8,8,8]{0,3,2,1:T(8,128)(2,1)}, u32[]{:S(2)}) copy-start(bf16[8,8,8,8]{0,3,2,1:T(8,128)(2,1)} %get-tuple-element.107) | copy-start | bytes 24580
  219.4 14.3 %copy-start.60 = (bf16[8,8,8,8]{0,3,2,1:T(8,128)(2,1)S(1)}, bf16[8,8,8,8]{0,3,2,1:T(8,128)(2,1)}, u32[]{:S(2)}) copy-start(bf16[8,8,8,8]{0,3,2,1:T(8,128)(2,1)} %get-tuple-element.108) | copy-start | bytes 24580
  220.5 14.3 %copy-start.59 = (bf16[8,8,8,8]{0,3,2,1:T(8,128)(2,1)S(1)}, bf16[8,8,8,8]{0,3,2,1:T(8,128)(2,1)}, u32[]{:S(2)}) copy-start(bf16[8,8,8,8]{0,3,2,1:T(8,128)(2,1)} %get-tuple-element.109) | copy-start | bytes 24580
  221.5 14.3 %copy-start.58 = (bf16[8,8,8,8]{0,3,2,1:T(8,128)(2,1)S(1)}, bf16[8,8,8,8]{0,3,2,1:T(8,128)(2,1)}, u32[]{:S(2)}) copy-start(bf16[8,8,8,8]{0,3,2,1:T(8,128)(2,1)} %get-tuple-element.102) | copy-start | bytes 24580
  222.6 14.3 %copy-start.57 = (bf16[8,8,8,8]{0,3,2,1:T(8,128)(2,1)S(1)}, bf16[8,8,8,8]{0,3,2,1:T(8,128)(2,1)}, u32[]{:S(2)}) copy-start(bf16[8,8,8,8]{0,3,2,1:T(8,128)(2,1)} %get-tuple-element.103) | copy-start | bytes 24580
  229.5 14.3 %copy-start.56 = (bf16[8,8,8,8]{0,3,2,1:T(8,128)(2,1)S(1)}, bf16[8,8,8,8]{0,3,2,1:T(8,128)(2,1)}, u32[]{:S(2)}) copy-start(bf16[8,8,8,8]{0,3,2,1:T(8,128)(2,1)} %get-tuple-element.99) | copy-start | bytes 24580
  230.6 14.3 %copy-start.55 = (bf16[8,8,8,8]{0,3,2,1:T(8,128)(2,1)S(1)}, bf16[8,8,8,8]{0,3,2,1:T(8,128)(2,1)}, u32[]{:S(2)}) copy-start(bf16[8,8,8,8]{0,3,2,1:T(8,128)(2,1)} %get-tuple-element.100) | copy-start | bytes 24580
  236.1 14.1 %copy-start.50 = (bf16[8,8,8,8]{0,3,2,1:T(8,128)(2,1)S(1)}, bf16[8,8,8,8]{0,3,2,1:T(8,128)(2,1)}, u32[]{:S(2)}) copy-start(bf16[8,8,8,8]{0,3,2,1:T(8,128)(2,1)} %get-tuple-element.97) | copy-start | bytes 24580
  247.3 14.1 %copy-start.45 = (bf16[8,8,8,8]{0,3,2,1:T(8,128)(2,1)S(1)}, bf16[8,8,8,8]{0,3,2,1:T(8,128)(2,1)}, u32[]{:S(2)}) copy-start(bf16[8,8,8,8]{0,3,2,1:T(8,128)(2,1)} %get-tuple-element.89) | copy-start | bytes 24580
  258.5 14.1 %copy-start.40 = (bf16[8,8,8,8]{0,3,2,1:T(8,128)(2,1)S(1)}, bf16[8,8,8,8]{0,3,2,1:T(8,128)(2,1)}, u32[]{:S(2)}) copy-start(bf16[8,8,8,8]{0,3,2,1:T(8,128)(2,1)} %get-tuple-element.81) | copy-start | bytes 24580
  259.6 14.1 %copy-start.39 = (bf16[8,8,8,8]{0,3,2,1:T(8,128)(2,1)S(1)}, bf16[8,8,8,8]{0,3,2,1:T(8,128)(2,1)}, u32[]{:S(2)}) copy-start(bf16[8,8,8,8]{0,3,2,1:T(8,128)(2,1)} %get-tuple-element.74) | copy-start | bytes 24580
  260.7 14.1 %copy-start.38 = (bf16[8,8,8,8]{0,3,2,1:T(8,128)(2,1)S(1)}, bf16[8,8,8,8]{0,3,2,1:T(8,128)(2,1)}, u32[]{:S(2)}) copy-start(bf16[8,8,8,8]{0,3,2,1:T(8,128)(2,1)} %get-tuple-element.75) | copy-start | bytes 24580
  261.7 14.1 %copy-start.37 = (bf16[8,8,8,8]{0,3,2,1:T(8,128)(2,1)S(1)}, bf16[8,8,8,8]{0,3,2,1:T(8,128)(2,1)}, u32[]{:S(2)}) copy-start(bf16[8,8,8,8]{0,3,2,1:T(8,128)(2,1)} %get-tuple-element.76) | copy-start | bytes 24580
  262.8 14.5 %copy-start.36 = (bf16[8,8,8,8]{0,3,2,1:T(8,128)(2,1)S(1)}, bf16[8,8,8,8]{0,3,2,1:T(8,128)(2,1)}, u32[]{:S(2)}) copy-start(bf16[8,8,8,8]{0,3,2,1:T(8,128)(2,1)} %get-tuple-element.77) | copy-start | bytes 24580
  263.9 14.5 %copy-start.35 = (bf16[8,8,8,8]{0,3,2,1:T(8,128)(2,1)S(1)}, bf16[8,8,8,8]{0,3,2,1:T(8,128)(2,1)}, u32[]{:S(2)}) copy-start(bf16[8,8,8,8]{0,3,2,1:T(8,128)(2,1)} %get-tuple-element.70) | copy-start | bytes 24580
  264.9 14.5 %copy-start.34 = (bf16[8,8,8,8]{0,3,2,1:T(8,128)(2,1)S(1)}, bf16[8,8,8,8]{0,3,2,1:T(8,128)(2,1)}, u32[]{:S(2)}) copy-start(bf16[8,8,8,8]{0,3,2,1:T(8,128)(2,1)} %get-tuple-element.71) | copy-start | bytes 24580
  266.0 14.5 %copy-start.33 = (bf16[8,8,8,8]{0,3,2,1:T(8,128)(2,1)S(1)}, bf16[8,8,8,8]{0,3,2,1:T(8,128)(2,1)}, u32[]{:S(2)}) copy-start(bf16[8,8,8,8]{0,3,2,1:T(8,128)(2,1)} %get-tuple-element.72) | copy-start | bytes 24580
  272.9 14.5 %copy-start.32 = (bf16[8,8,8,8]{0,3,2,1:T(8,128)(2,1)S(1)}, bf16[8,8,8,8]{0,3,2,1:T(8,128)(2,1)}, u32[]{:S(2)}) copy-start(bf16[8,8,8,8]{0,3,2,1:T(8,128)(2,1)} %get-tuple-element.68) | copy-start | bytes 24580
  274.0 14.5 %copy-start.31 = (bf16[8,8,8,8]{0,3,2,1:T(8,128)(2,1)S(1)}, bf16[8,8,8,8]{0,3,2,1:T(8,128)(2,1)}, u32[]{:S(2)}) copy-start(bf16[8,8,8,8]{0,3,2,1:T(8,128)(2,1)} %get-tuple-element.69) | copy-start | bytes 24580
  275.1 14.5 %copy-start.30 = (bf16[8,8,8,8]{0,3,2,1:T(8,128)(2,1)S(1)}, bf16[8,8,8,8]{0,3,2,1:T(8,128)(2,1)}, u32[]{:S(2)}) copy-start(bf16[8,8,8,8]{0,3,2,1:T(8,128)(2,1)} %get-tuple-element.62) | copy-start | bytes 24580
  276.1 14.5 %copy-start.29 = (bf16[8,8,8,8]{0,3,2,1:T(8,128)(2,1)S(1)}, bf16[8,8,8,8]{0,3,2,1:T(8,128)(2,1)}, u32[]{:S(2)}) copy-start(bf16[8,8,8,8]{0,3,2,1:T(8,128)(2,1)} %get-tuple-element.63) | copy-start | bytes 24580
  277.6 14.1 %copy-start.28 = (bf16[8,8,8,8]{0,3,2,1:T(8,128)(2,1)S(1)}, bf16[8,8,8,8]{0,3,2,1:T(8,128)(2,1)}, u32[]{:S(2)}) copy-start(bf16[8,8,8,8]{0,3,2,1:T(8,128)(2,1)} %get-tuple-element.64) | copy-start | bytes 24580
  279.7 14.1 %copy-start.26 = (bf16[8,8,8,8]{0,3,2,1:T(8,128)(2,1)S(1)}, bf16[8,8,8,8]{0,3,2,1:T(8,128)(2,1)}, u32[]{:S(2)}) copy-start(bf16[8,8,8,8]{0,3,2,1:T(8,128)(2,1)} %get-tuple-element.58) | copy-start | bytes 24580
  287.7 14.1 %copy-start.24 = (bf16[8,8,8,8]{0,3,2,1:T(8,128)(2,1)S(1)}, bf16[8,8,8,8]{0,3,2,1:T(8,128)(2,1)}, u32[]{:S(2)}) copy-start(bf16[8,8,8,8]{0,3,2,1:T(8,128)(2,1)} %get-tuple-element.55) | copy-start | bytes 24580
  288.8 14.1 %copy-start.23 = (bf16[8,8,8,8]{0,3,2,1:T(8,128)(2,1)S(1)}, bf16[8,8,8,8]{0,3,2,1:T(8,128)(2,1)}, u32[]{:S(2)}) copy-start(bf16[8,8,8,8]{0,3,2,1:T(8,128)(2,1)} %get-tuple-element.56) | copy-start | bytes 24580
  289.8 14.1 %copy-start.22 = (bf16[8,8,8,8]{0,3,2,1:T(8,128)(2,1)S(1)}, bf16[8,8,8,8]{0,3,2,1:T(8,128)(2,1)}, u32[]{:S(2)}) copy-start(bf16[8,8,8,8]{0,3,2,1:T(8,128)(2,1)} %get-tuple-element.57) | copy-start | bytes 24580
  290.9 14.1 %copy-start.21 = (bf16[8,8,8,8]{0,3,2,1:T(8,128)(2,1)S(1)}, bf16[8,8,8,8]{0,3,2,1:T(8,128)(2,1)}, u32[]{:S(2)}) copy-start(bf16[8,8,8,8]{0,3,2,1:T(8,128)(2,1)} %get-tuple-element.50) | copy-start | bytes 24580
  292.0 14.1 %copy-start.20 = (bf16[8,8,8,8]{0,3,2,1:T(8,128)(2,1)S(1)}, bf16[8,8,8,8]{0,3,2,1:T(8,128)(2,1)}, u32[]{:S(2)}) copy-start(bf16[8,8,8,8]{0,3,2,1:T(8,128)(2,1)} %get-tuple-element.51) | copy-start | bytes 24580
  293.0 14.1 %copy-start.19 = (bf16[8,8,8,8]{0,3,2,1:T(8,128)(2,1)S(1)}, bf16[8,8,8,8]{0,3,2,1:T(8,128)(2,1)}, u32[]{:S(2)}) copy-start(bf16[8,8,8,8]{0,3,2,1:T(8,128)(2,1)} %get-tuple-element.52) | copy-start | bytes 24580
  294.1 14.1 %copy-start.18 = (bf16[8,8,8,8]{0,3,2,1:T(8,128)(2,1)S(1)}, bf16[8,8,8,8]{0,3,2,1:T(8,128)(2,1)}, u32[]{:S(2)}) copy-start(bf16[8,8,8,8]{0,3,2,1:T(8,128)(2,1)} %get-tuple-element.53) | copy-start | bytes 24580
  295.2 14.1 %copy-start.17 = (bf16[8,8,8,8]{0,3,2,1:T(8,128)(2,1)S(1)}, bf16[8,8,8,8]{0,3,2,1:T(8,128)(2,1)}, u32[]{:S(2)}) copy-start(bf16[8,8,8,8]{0,3,2,1:T(8,128)(2,1)} %get-tuple-element.46) | copy-start | bytes 24580
  308.5 14.3 %copy-start.10 = (bf16[8,8,8,8]{0,3,2,1:T(8,128)(2,1)S(1)}, bf16[8,8,8,8]{0,3,2,1:T(8,128)(2,1)}, u32[]{:S(2)}) copy-start(bf16[8,8,8,8]{0,3,2,1:T(8,128)(2,1)} %get-tuple-element.40) | copy-start | bytes 24580
  309.6 14.3 %copy-start.9 = (bf16[8,8,8,8]{0,3,2,1:T(8,128)(2,1)S(1)}, bf16[8,8,8,8]{0,3,2,1:T(8,128)(2,1)}, u32[]{:S(2)}) copy-start(bf16[8,8,8,8]{0,3,2,1:T(8,128)(2,1)} %get-tuple-element.41) | copy-start | bytes 24580
  317.6 15.2 %copy-start.8 = (bf16[8,8,8,8]{0,3,2,1:T(8,128)(2,1)S(1)}, bf16[8,8,8,8]{0,3,2,1:T(8,128)(2,1)}, u32[]{:S(2)}) copy-start(bf16[8,8,8,8]{0,3,2,1:T(8,128)(2,1)} %get-tuple-element.30) | copy-start | bytes 24580
  318.6 15.2 %copy-start.7 = (bf16[8,8,8,8]{0,3,2,1:T(8,128)(2,1)S(1)}, bf16[8,8,8,8]{0,3,2,1:T(8,128)(2,1)}, u32[]{:S(2)}) copy-start(bf16[8,8,8,8]{0,3,2,1:T(8,128)(2,1)} %get-tuple-element.31) | copy-start | bytes 24580
  319.7 15.2 %copy-start.6 = (bf16[8,8,8,8]{0,3,2,1:T(8,128)(2,1)S(1)}, bf16[8,8,8,8]{0,3,2,1:T(8,128)(2,1)}, u32[]{:S(2)}) copy-start(bf16[8,8,8,8]{0,3,2,1:T(8,128)(2,1)} %get-tuple-element.32) | copy-start | bytes 24580
  320.8 15.1 %copy-start.5 = (bf16[8,8,8,8]{0,3,2,1:T(8,128)(2,1)S(1)}, bf16[8,8,8,8]{0,3,2,1:T(8,128)(2,1)}, u32[]{:S(2)}) copy-start(bf16[8,8,8,8]{0,3,2,1:T(8,128)(2,1)} %get-tuple-element.33) | copy-start | bytes 24580
  322.0 15.0 %copy-start.4 = (bf16[8,8,8,8]{0,3,2,1:T(8,128)(2,1)S(1)}, bf16[8,8,8,8]{0,3,2,1:T(8,128)(2,1)}, u32[]{:S(2)}) copy-start(bf16[8,8,8,8]{0,3,2,1:T(8,128)(2,1)} %get-tuple-element.26) | copy-start | bytes 24580
  323.1 15.0 %copy-start.3 = (bf16[8,8,8,8]{0,3,2,1:T(8,128)(2,1)S(1)}, bf16[8,8,8,8]{0,3,2,1:T(8,128)(2,1)}, u32[]{:S(2)}) copy-start(bf16[8,8,8,8]{0,3,2,1:T(8,128)(2,1)} %get-tuple-element.27) | copy-start | bytes 24580
  324.1 14.9 %copy-start.2 = (bf16[8,8,8,8]{0,3,2,1:T(8,128)(2,1)S(1)}, bf16[8,8,8,8]{0,3,2,1:T(8,128)(2,1)}, u32[]{:S(2)}) copy-start(bf16[8,8,8,8]{0,3,2,1:T(8,128)(2,1)} %get-tuple-element.28) | copy-start | bytes 24580
  (78 other events, 663.1 us)
Sparse Core Ops, SparseCore 0:
  372.7 940.5 all-gather.4
